TPU v7x, 32 devices: a whole 2x2x4 slice. The times are simulated.
32 devices in a mesh: cfg: 2 (over core), req: 16 (over z, y, x).
Axes of the slice: x: 2, y: 2, z: 4, core: 2. Of those that a mesh axis runs over, the one named last changes fastest.
Arguments:
- query_rows: bfloat16 [2, 8192, 2560], P('cfg', 'req'), may hold values from -32 to 32
- key_rows: bfloat16 [2, 8192, 2560], P('cfg', 'req'), may hold values from -6 to 6
- value_rows: bfloat16 [2, 8192, 2560], P('cfg', 'req'), may hold values from -600 to 600
- positions: int32 [3, 8192], P(None, 'req'), may hold values from 0 to 51
- latents: float32 [8192, 64], P('req', 'cfg'), may hold values from -6 to 6
- w_head: bfloat16 [2560, 64], replicated, may hold values from -0.125 to 0.125
- modulation: float32 [2, 2560], replicated, may hold values from -0.5 to 1
- guide_scale: float32 [1], replicated, may hold values from 4 to 6
- step_sizes: float32 [32], replicated, may hold values from -0.4 to -0.1
- lengths: int32 [32], replicated, may hold values from 1 to 512, 8192 in all
Outputs:
- next_latents: float32 [8192, 64], P('req', 'cfg')
Inputs may be any that keep to these rules, and one draw needn't show every extreme that they name: Videos are laid end to end in the given order and their lengths sum to 8192.
All inputs are finite; a program needn't handle non-finite values.
Results may differ from a plain program's by a relative error of at most 0.0059.
Values may be sent and summed in bfloat16 or wider, within the bound.
No kernel may reach another device: no remote copies, remote signals or barrier semaphores. Data moves between devices by JAX's collectives and lax.ppermute only.
A program may use at most 128 MiB of HBM per device.

v0:
```python
import math

import jax
import jax.numpy as jnp
from jax import lax
from jax.sharding import PartitionSpec as P

HD = 128
LMAX = 512


masked_score = -1e30
rope_theta = 10000.0


def extended(cells, sides, width):
    for axis, dim in sides:
        count = lax.axis_size(axis)
        ends = count - 1
        head = lax.slice_in_dim(cells, 0, width, axis=dim)
        tail = lax.slice_in_dim(cells, cells.shape[dim] - width, cells.shape[dim], axis=dim)
        cells = jnp.concatenate(
            [
                lax.ppermute(tail, axis, [(i, (i + 1) % count) for i in range(ends)]),
                cells,
                lax.ppermute(head, axis, [((i + 1) % count, i) for i in range(ends)]),
            ],
            axis=dim,
        )
    return cells


def from_partner(x, axis, distance):
    return lax.ppermute(x, axis, [(i, i ^ 1 << distance) for i in range(lax.axis_size(axis))])


def angles(positions):
    pair_total = HD // 2
    side_pairs = HD // 6
    time_pairs = pair_total - 2 * side_pairs
    column = jnp.arange(pair_total, dtype=jnp.int32)
    in_time = column < time_pairs
    in_height = (column >= time_pairs) & (column < time_pairs + side_pairs)
    in_width = column >= time_pairs + side_pairs
    local_index = jnp.where(
        in_time, column, jnp.where(in_height, column - time_pairs, column - time_pairs - side_pairs)
    )
    axis_pairs = jnp.where(in_time, time_pairs, side_pairs)
    frequency = jnp.exp(
        -(local_index.astype(jnp.float32) / axis_pairs.astype(jnp.float32)) * math.log(rope_theta)
    )
    selector = jnp.stack([in_time, in_height, in_width]).astype(jnp.float32) * frequency[None, :]
    placed = positions.astype(jnp.float32)
    return (
        placed[0][:, None] * selector[0][None, :]
        + placed[1][:, None] * selector[1][None, :]
        + placed[2][:, None] * selector[2][None, :]
    )


def rotate(features, angle_table):
    row_total = features.shape[0]
    heads_here = features.shape[1] // HD
    paired = features.astype(jnp.float32).reshape(row_total, heads_here, HD // 2, 2)
    cosine = jnp.cos(angle_table)[:, None, :]
    sine_part = jnp.sin(angle_table)[:, None, :]
    real_part = paired[..., 0]
    imag_part = paired[..., 1]
    turned = jnp.stack(
        [real_part * cosine - imag_part * sine_part, real_part * sine_part + imag_part * cosine],
        axis=-1,
    )
    return turned.reshape(row_total, heads_here * HD).astype(jnp.bfloat16)


def video_of(global_rows, video_ends, row_count):
    inside = (global_rows >= 0) & (global_rows < row_count)
    counted = jnp.sum((video_ends[None, :] <= global_rows[:, None]).astype(jnp.int32), axis=1)
    return jnp.where(inside, counted, -1)


def attend_masked(query_block, key_block, value_block, query_video, key_video):
    rows_here = query_block.shape[0]
    feature_count = query_block.shape[1]
    heads_here = feature_count // HD
    key_count = key_block.shape[0]
    same_video = query_video[:, None] == key_video[None, :]
    score_scale = 1.0 / math.sqrt(HD)
    query_heads = query_block.reshape(rows_here, heads_here, HD).transpose(1, 0, 2)
    key_heads = key_block.reshape(key_count, heads_here, HD).transpose(1, 0, 2)
    value_heads = value_block.reshape(key_count, heads_here, HD).transpose(1, 0, 2)

    def one_head(operands):
        query_head, key_head, value_head = operands
        scores = jnp.dot(query_head, key_head.T, preferred_element_type=jnp.float32) * score_scale
        scores = jnp.where(same_video, scores, masked_score)
        row_max = jnp.max(scores, axis=1, keepdims=True)
        weights = jnp.exp(scores - row_max)
        denominator = jnp.sum(weights, axis=1, keepdims=True)
        summed = jnp.dot(
            weights.astype(jnp.bfloat16), value_head, preferred_element_type=jnp.float32
        )
        return (summed / denominator).astype(jnp.bfloat16)

    outputs = lax.map(one_head, (query_heads, key_heads, value_heads))
    return outputs.transpose(1, 0, 2).reshape(rows_here, feature_count)


def project(attended, modulation, w_head):
    widened = attended.astype(jnp.float32)
    mean_square = jnp.mean(widened * widened, axis=1, keepdims=True)
    normed = (
        widened * lax.rsqrt(mean_square + 1e-06) * (1.0 + modulation[1][None, :])
        + modulation[0][None, :]
    )
    return jnp.dot(normed.astype(jnp.bfloat16), w_head, preferred_element_type=jnp.float32)


def step_rows(video_ids, step_sizes):
    video_count = step_sizes.shape[0]
    chosen = video_ids[:, None] == jnp.arange(video_count, dtype=jnp.int32)[None, :]
    return jnp.sum(
        jnp.where(chosen, step_sizes[None, :], jnp.zeros_like(step_sizes)[None, :]), axis=1
    )


def per_device(
    query_rows,
    key_rows,
    value_rows,
    positions,
    latents,
    w_head,
    modulation,
    guide_scale,
    step_sizes,
    lengths,
):
    rows_here = query_rows.shape[1]
    feature_count = query_rows.shape[2]
    row_count = rows_here * lax.axis_size("req")
    first_row = lax.axis_index("req") * rows_here
    angle_table = angles(positions)
    video_ends = jnp.cumsum(lengths)
    query_rot = rotate(query_rows[0], angle_table)
    key_rot = rotate(key_rows[0], angle_table)
    joined = jnp.concatenate([key_rot, value_rows[0]], axis=1)
    window = extended(joined, (("req", 0),), LMAX)
    query_video = video_of(
        first_row + jnp.arange(rows_here, dtype=jnp.int32), video_ends, row_count
    )
    key_video = video_of(
        first_row - LMAX + jnp.arange(rows_here + 2 * LMAX, dtype=jnp.int32), video_ends, row_count
    )
    attended = attend_masked(
        query_rot, window[:, :feature_count], window[:, feature_count:], query_video, key_video
    )
    velocity = project(attended, modulation, w_head)
    parity = lax.axis_index("cfg")
    video_ids = video_of(first_row + jnp.arange(rows_here, dtype=jnp.int32), video_ends, row_count)
    steps_here = step_rows(video_ids, step_sizes)
    half_cols = latents.shape[1]
    own_start = parity * half_cols
    partner = from_partner(velocity, "cfg", 0)
    conditional = jnp.where(parity == 0, velocity, partner)
    unconditional = jnp.where(parity == 0, partner, velocity)
    guided = unconditional + guide_scale[0] * (conditional - unconditional)
    own_guided = lax.dynamic_slice_in_dim(guided, own_start, half_cols, 1)
    return latents + steps_here[:, None] * own_guided


def solution(mesh):
    in_specs = (
        P("cfg", "req", None),
        P("cfg", "req", None),
        P("cfg", "req", None),
        P(None, "req"),
        P("req", "cfg"),
        P(),
        P(),
        P(),
        P(),
        P(),
    )
    out_specs = P("req", "cfg")
    return jax.shard_map(
        per_device, mesh=mesh, in_specs=in_specs, out_specs=out_specs, check_vma=False
    )
```

profile of v0, /device:TPU:17, one launch (start us, length us, event | category | flops | bytes accessed | tf_op | source)
XLA Modules:
  0.0 409.8 jit_solution(17010585596311361380)
XLA Ops:
  0.8 4.9 %copy.26 = f32[1,512,2560]{1,2,0:T(8,128)} copy(bf16[1,512,2560]{2,1,0:T(8,128)(2,1)} %param.12) | data formatting | bytes 7864320 | tf_op jit(solution)/shard_map/convert_element_type | solution.py:64
  5.7 7.7 %reshape.297 = f32[512,20,64,2]{0,3,2,1:T(2,128)} reshape(f32[1,512,2560]{1,2,0:T(8,128)} %copy.26) | data formatting | bytes 10485760 | tf_op jit(solution)/shard_map/convert_element_type | solution.py:64
  13.4 3.2 copy.27
  16.6 7.6 %reshape.298 = f32[512,20,64,2]{0,3,2,1:T(2,128)} reshape(f32[1,512,2560]{1,2,0:T(8,128)} %copy.27) | data formatting | bytes 10485760 | tf_op jit(solution)/shard_map/convert_element_type | solution.py:64
  24.7 16.5 %subtract_convert_fusion = (bf16[512,20,64,1]{0,3,2,1:T(2,128)(2,1)S(1)}, bf16[512,20,64,1]{0,3,2,1:T(2,128)(2,1)S(1)}, bf16[512,20,64,1]{0,3,2,1:T(2,128)(2,1)}, bf16[512,20,64,1]{0,3,2,1:T(2,128)(2,1)}) fusion(f32[512,20,64,2]{0,3,2,1:T(2,128)} %reshape.298, f32[512,64]{0,1:T(8,128)S(1)} %get-tuple-element.100, f32[512,64]{0,1:T(8,128)S(1)} %get-tuple-element.99, ...), kind=kLoop, calls=%fused_computation.30 | loop fusion | flops 10485760 | bytes 15990784 | tf_op jit(solution)/shard_map/convert.4
  41.3 6.3 %pad_maximum_fusion.3 = bf16[512,20,64,2]{0,3,2,1:T(2,128)(2,1)} fusion(bf16[512,20,64,1]{0,3,2,1:T(2,128)(2,1)S(1)} %get-tuple-element.91, bf16[512,20,64,1]{0,3,2,1:T(2,128)(2,1)S(1)} %get-tuple-element.90), kind=kLoop, calls=%fused_computation.28 | loop fusion | flops 5242880 | bytes 5242880 | tf_op jit(solution)/shard_map/stack | solution.py:69
  47.6 3.8 convert_element_type.79
  51.3 4.5 %copy.28 = bf16[1,512,2560]{1,2,0:T(8,128)(2,1)} copy(bf16[1,512,2560]{2,1,0:T(8,128)(2,1)} %param.14) | data formatting | bytes 5242880 | tf_op args[2]
  55.8 4.4 %pad_maximum_fusion.1 = bf16[512,5120]{0,1:T(8,128)(2,1)} fusion(bf16[512,2560]{0,1:T(8,128)(2,1)} %bitcast.66, bf16[512,2560]{0,1:T(8,128)(2,1)S(1)} %convert_element_type.79), kind=kLoop, calls=%fused_computation.21 | loop fusion | flops 10485760 | bytes 10485760 | tf_op jit(solution)/shard_map/concatenate | solution.py:147
  60.3 3.1 collective-permute-start
  63.4 4.1 %collective-permute-start.1 = (bf16[512,5120]{0,1:T(8,128)(2,1)}, bf16[512,5120]{0,1:T(8,128)(2,1)}, u32[]{:S(2)}, u32[]{:S(2)}) collective-permute-start(bf16[512,5120]{0,1:T(8,128)(2,1)} %pad_maximum_fusion.1), channel_id=1, source_target_pairs={{1,0},{2,1},{3,2},{4,3},{5,4},{6,5},{7,6},{8,7},{9,8},{10,9},{11,1... | collective-permute-start | bytes 15728648 | tf_op jit(solution)/shard_map/ppermute | solution.py:26
  67.5 8.1 %pad_maximum_fusion.2 = bf16[512,20,64,2]{0,3,2,1:T(2,128)(2,1)} fusion(bf16[512,20,64,1]{0,3,2,1:T(2,128)(2,1)} %get-tuple-element.94, bf16[512,20,64,1]{0,3,2,1:T(2,128)(2,1)} %get-tuple-element.95), kind=kLoop, calls=%fused_computation.27 | loop fusion | flops 5242880 | bytes 5242880 | tf_op jit(solution)/shard_map/stack | solution.py:69
  75.6 5.1 %convert_element_type.76 = bf16[512,20,128]{0,2,1:T(8,128)(2,1)} reshape(bf16[512,20,64,2]{0,3,2,1:T(2,128)(2,1)} %pad_maximum_fusion.2) | data formatting | bytes 5242880 | tf_op jit(solution)/shard_map/convert_element_type | solution.py:73
  81.3 206.4 %collective-permute-done = bf16[512,5120]{0,1:T(8,128)(2,1)} collective-permute-done((bf16[512,5120]{0,1:T(8,128)(2,1)}, bf16[512,5120]{0,1:T(8,128)(2,1)}, u32[]{:S(2)}, u32[]{:S(2)}) %collective-permute-start) | collective-permute-done | bytes 5242912 | tf_op jit(solution)/shard_map/ppermute | solution.py:24
  287.7 1.9 collective-permute-done.1
  289.7 23.7 %pad_maximum_fusion = bf16[1536,5120]{0,1:T(8,128)(2,1)S(1)} fusion(bf16[512,5120]{0,1:T(8,128)(2,1)} %collective-permute-done.1, bf16[512,2560]{0,1:T(8,128)(2,1)} %bitcast.67, bf16[512,2560]{0,1:T(8,128)(2,1)S(1)} %convert_element_type.79, bf16[512,5120]{0,1:T(8,128)(2,1)} %collective-permute-done), kind=kLoop, calls=%fused_computation.20 | loop fusion | flops 62914560 | bytes 31457280 | tf_op jit(solution)/shard_map/concatenate | solution.py:22
  313.4 5.8 %fusion.37 = (bf16[1536,2560]{0,1:T(8,128)(2,1)}, bf16[1536,2560]{0,1:T(8,128)(2,1)}) fusion(bf16[1536,5120]{0,1:T(8,128)(2,1)S(1)} %pad_maximum_fusion), kind=kLoop, calls=%fused_computation.67 | loop fusion | bytes 31457280 | tf_op jit(solution)/shard_map/slice | solution.py:156
  319.2 84.7 %while.11 = (s32[]{:T(128)}, bf16[20,512,128]{1,2,0:T(8,128)(2,1)S(1)}, bf16[20,512,128]{1,2,0:T(8,128)(2,1)}, bf16[20,1536,128]{1,2,0:T(8,128)(2,1)}, bf16[20,1...) while((s32[]{:T(128)}, bf16[20,512,128]{1,2,0:T(8,128)(2,1)S(1)}, ...), condition=%wide.region_7.8_spmd.clone, body=%wide.region_4.7_spmd.clone.sunk | while | flops 409074688 | bytes 11030105 | solution.py:105
  323.4 1.9 fusion.49
  327.6 1.9 fusion.49
  331.9 1.9 fusion.49
  336.1 1.9 fusion.49
  378.5 1.9 fusion.49
  386.9 1.9 fusion.49
  (135 shorter events, 80.0 us)
Async XLA Ops:
  0.0 406.0 %copy-start = (bf16[2560,64]{0,1:T(8,128)(2,1)S(1)}, bf16[2560,64]{0,1:T(8,128)(2,1)}, u32[]{:S(2)}) copy-start(bf16[2560,64]{0,1:T(8,128)(2,1)} %param.17) | copy-start | bytes 983044
  5.7 7.7 %copy-start.2 = (bf16[1,512,2560]{2,1,0:T(8,128)(2,1)S(1)}, bf16[1,512,2560]{2,1,0:T(8,128)(2,1)}, u32[]{:S(2)}) copy-start(bf16[1,512,2560]{2,1,0:T(8,128)(2,1)} %param.13) | copy-start | bytes 7864324
  60.3 227.5 %collective-permute-start = (bf16[512,5120]{0,1:T(8,128)(2,1)}, bf16[512,5120]{0,1:T(8,128)(2,1)}, u32[]{:S(2)}, u32[]{:S(2)}) collective-permute-start(bf16[512,5120]{0,1:T(8,128)(2,1)} %pad_maximum_fusion.1), channel_id=1, source_target_pairs={{0,1},{1,2},{2,3},{3,4},{4,5},{5,6},{6,7},{7,8},{8,9},{9,10},{10,1... | collective-permute-start | bytes 15728648 | tf_op jit(solution)/shard_map/ppermute | solution.py:24
  63.4 226.3 %collective-permute-start.1 = (bf16[512,5120]{0,1:T(8,128)(2,1)}, bf16[512,5120]{0,1:T(8,128)(2,1)}, u32[]{:S(2)}, u32[]{:S(2)}) collective-permute-start(bf16[512,5120]{0,1:T(8,128)(2,1)} %pad_maximum_fusion.1), channel_id=1, source_target_pairs={{1,0},{2,1},{3,2},{4,3},{5,4},{6,5},{7,6},{8,7},{9,8},{10,9},{11,1... | collective-permute-start | bytes 15728648 | tf_op jit(solution)/shard_map/ppermute | solution.py:26
  75.6 5.2 %copy-start.5 = (s32[32]{0:T(128)S(1)}, s32[32]{0:T(128)}, u32[]{:S(2)}) copy-start(s32[32]{0:T(128)} %param.21) | copy-start | bytes 388
  75.6 5.6 %copy-start.4 = (f32[2,2560]{1,0:T(2,128)S(1)}, f32[2,2560]{1,0:T(2,128)}, u32[]{:S(2)}) copy-start(f32[2,2560]{1,0:T(2,128)} %param.18) | copy-start | bytes 61444
  313.4 5.8 %copy-start.1 = (bf16[20,512,128]{1,2,0:T(8,128)(2,1)S(1)}, bf16[20,512,128]{1,2,0:T(8,128)(2,1)}, u32[]{:S(2)}) copy-start(bf16[20,512,128]{1,2,0:T(8,128)(2,1)} %custom-call) | copy-start | bytes 7864324
  404.5 4.3 %copy-start.6 = (f32[32]{0:T(128)S(1)}, f32[32]{0:T(128)}, u32[]{:S(2)}) copy-start(f32[32]{0:T(128)} %param.20) | copy-start | bytes 388
  404.5 4.6 %copy-start.3 = (f32[512,32]{0,1:T(8,128)S(1)}, f32[512,32]{0,1:T(8,128)}, u32[]{:S(2)}) copy-start(f32[512,32]{0,1:T(8,128)} %param.16) | copy-start | bytes 196612
  406.6 2.6 collective-permute-start.2
where the time goes:
time: 413 us; the launch traced here: 410 us
  waiting for transfers between devices  209 us (51%)
  other arithmetic  75.1 us (18%)
  matrix products  70.5 us (17%)
  local copies, waits for them, and re-layouts  45.3 us (11%)
  starting transfers between devices  8.86 us (2%)
    ppermute x1, waiting for transfers between devices, extended(): lax.ppermute(tail, axis, [(i, (i + 1) % count) for i in range(ends)])  206 us
    dot_general x20, matrix products, one_head(): jnp.dot(query_head, key_head.T, preferred_element_type=jnp.float32)  37.1 us
    dot_general x20, matrix products, one_head(): jnp.dot(weights.astype(jnp.bfloat16), value_head, preferred_element_type=...  32.8 us
    concatenate x1, other arithmetic, extended(): jnp.concatenate([lax.ppermute(tail, axis, [(i, (i + 1) % count) for i in...  23.7 us
    convert_element_type x4, local copies, waits for them, and re-layouts, rotate(): features.astype(jnp.float32).reshape(row_total, heads_here, HD // 2, 2)  23.4 us
    another operation x3, other arithmetic  16.7 us
    another operation x2, other arithmetic, rotate(): jnp.stack([real_part * cosine - imag_part * sine_part, real_part * sine_p...  14.4 us
    reduce_sum x20, other arithmetic, one_head(): denominator = jnp.sum(weights, axis=1, keepdims=True)  11.5 us
  transfers between devices with their start and end apart: 3, of which 3 were waited for; matrix products, arithmetic and copies ran while one was open for 3% of the time, Pallas kernels for 0%

commit v1 on v0

v1 whole, which is shorter than its diff:
```python
import functools
import math

import jax
import jax.numpy as jnp
from jax import lax
from jax.experimental import pallas as pl
from jax.experimental.pallas import tpu as pltpu
from jax.sharding import PartitionSpec as P

HD = 128
TILE = 16
BLK = 128
rope_theta = 10000.0
NEG = -1e30
SCALE2 = math.log2(math.e) / math.sqrt(HD)
VMEM_LIMIT = 56 * 1024 * 1024

L_TILES, L_OWN_TILES, L_HEADS, L_FAR, L_OWN = 0, 1, 2, 3, 4
R_TILES, R_OWN_TILES, R_HEADS, R_FAR, R_OWN = 5, 6, 7, 8, 9


def angles(positions):
    pair_total = HD // 2
    side_pairs = HD // 6
    time_pairs = pair_total - 2 * side_pairs
    column = jnp.arange(HD, dtype=jnp.int32) // 2
    in_time = column < time_pairs
    in_height = (column >= time_pairs) & (column < time_pairs + side_pairs)
    in_width = column >= time_pairs + side_pairs
    local_index = jnp.where(
        in_time, column, jnp.where(in_height, column - time_pairs, column - time_pairs - side_pairs)
    )
    axis_pairs = jnp.where(in_time, time_pairs, side_pairs)
    frequency = jnp.exp(
        -(local_index.astype(jnp.float32) / axis_pairs.astype(jnp.float32)) * math.log(rope_theta)
    )
    selector = jnp.stack([in_time, in_height, in_width]).astype(jnp.float32) * frequency[None, :]
    placed = positions.astype(jnp.float32)
    return (
        placed[0][:, None] * selector[0][None, :]
        + placed[1][:, None] * selector[1][None, :]
        + placed[2][:, None] * selector[2][None, :]
    )


def boundary(at, row_count, ends, starts, heads):
    inside = (starts < at) & (ends > at)
    left = jnp.sum(jnp.where(inside, at - starts, 0))
    right = jnp.sum(jnp.where(inside, ends - at, 0))
    left_tiles = (left + TILE - 1) // TILE
    right_tiles = (right + TILE - 1) // TILE
    choice = jnp.arange(heads + 1, dtype=jnp.int32)
    load = jnp.maximum(left_tiles * choice, right_tiles * (heads - choice))
    best = jnp.argmin(load).astype(jnp.int32)
    return left, right, left_tiles, right_tiles, best


def dot_t(a, b):
    return lax.dot_general(a, b, (((1,), (1,)), ((), ())), preferred_element_type=jnp.float32)


def prep_kernel(scal, q_ref, k_ref, v_ref, cos_ref, sin_ref, qr_ref, kr_ref, xl_ref, xr_ref):
    h = pl.program_id(0)
    rows = q_ref.shape[0]
    even = lax.rem(lax.broadcasted_iota(jnp.int32, (rows, HD), 1), 2) == 0

    def turn(ref):
        x = ref[...].astype(jnp.float32)
        swapped = jnp.where(even, pltpu.roll(x, HD - 1, 1), pltpu.roll(x, 1, 1))
        return (x * cos_ref[...] + swapped * sin_ref[...]).astype(jnp.bfloat16)

    qr_ref[...] = turn(q_ref)
    kr_ref[...] = turn(k_ref)

    def send(out_ref, tiles, slot, first_row):
        def one(t, carry):
            at = pl.multiple_of(first_row + t * TILE, TILE)
            item = slot * tiles + t
            out_ref[item, 0:TILE] = qr_ref[pl.ds(at, TILE), :]
            out_ref[item, TILE : 2 * TILE] = kr_ref[pl.ds(at, TILE), :]
            out_ref[item, 2 * TILE : 3 * TILE] = v_ref[pl.ds(at, TILE), :]
            return carry

        lax.fori_loop(0, tiles, one, 0)

    @pl.when(h >= scal[L_HEADS])
    def _():
        send(xl_ref, scal[L_OWN_TILES], h - scal[L_HEADS], 0)

    @pl.when(h < scal[R_HEADS])
    def _():
        send(xr_ref, scal[R_OWN_TILES], h, rows - TILE * scal[R_OWN_TILES])


def attend_rows(q, k, v_ones, scores_of):
    s = scores_of(dot_t(q, k) * SCALE2)
    top = jnp.max(s, axis=1, keepdims=True)
    weight = jnp.exp2(s - top).astype(jnp.bfloat16)
    both = jnp.dot(weight, v_ones, preferred_element_type=jnp.float32)
    return (both[:, :HD] / both[:, HD:]).astype(jnp.bfloat16)


def with_total(z, sq, keep):
    added = z + pltpu.roll(z, HD // 2, 1)
    lane = lax.broadcasted_iota(jnp.int32, z.shape, 1)
    total = jnp.sum(sq, axis=1, keepdims=True)
    out = jnp.where(lane < HD // 2, added, jnp.where(lane == HD // 2, total, 0.0))
    return jnp.where(keep, out, 0.0)


def local_kernel(scal, q_ref, k_ref, v_ref, w_ref, qv_ref, kv_ref, out_ref, z_ref, sq_ref):
    h = pl.program_id(0)
    rows = q_ref.shape[0]

    @pl.when(h == 0)
    def _():
        z_ref[...] = jnp.zeros_like(z_ref)
        sq_ref[...] = jnp.zeros_like(sq_ref)

    k = k_ref[...]
    v_ones = jnp.concatenate([v_ref[...], jnp.ones((rows, HD), jnp.bfloat16)], axis=1)
    for j in range(rows // BLK):
        at = pl.ds(j * BLK, BLK)
        same = qv_ref[at, :] == kv_ref[...]
        o = attend_rows(q_ref[at, :], k, v_ones, lambda s: jnp.where(same, s, NEG))
        z_ref[at, :] += jnp.dot(o, w_ref[...], preferred_element_type=jnp.float32)
        wide = o.astype(jnp.float32)
        sq_ref[at, :] += wide * wide

    @pl.when(h == pl.num_programs(0) - 1)
    def _():
        row = lax.broadcasted_iota(jnp.int32, (rows, HD), 0)
        keep = (row >= scal[L_OWN]) & (row < rows - scal[R_OWN])
        out_ref[...] = with_total(z_ref[...], sq_ref[...], keep)


def straddle_kernel(
    scal, q_ref, k_ref, v_ref, xl_ref, xr_ref, w_ref, own_ref, toleft_ref, toright_ref, qs, ks, vs, zs, ss
):
    h = pl.program_id(0)
    rows = q_ref.shape[0]
    span = ks.shape[1]

    @pl.when(h == 0)
    def _():
        for side in range(2):
            qs[side] = jnp.zeros_like(qs[side])
            ks[side] = jnp.zeros_like(ks[side])
            vs[side, :, :HD] = jnp.zeros((span, HD), jnp.bfloat16)
            vs[side, :, HD:] = jnp.ones((span, HD), jnp.bfloat16)
            zs[side] = jnp.zeros_like(zs[side])
            ss[side] = jnp.zeros_like(ss[side])

    def work(side, x_ref, far_tiles, slot, own_at, far_at, left, right):
        qs[side, pl.ds(own_at, rows)] = q_ref[...]
        ks[side, pl.ds(own_at, rows)] = k_ref[...]
        vs[side, pl.ds(own_at, rows), :HD] = v_ref[...]

        def one(t, carry):
            at = pl.ds(pl.multiple_of(far_at + t * TILE, TILE), TILE)
            item = slot * far_tiles + t
            qs[side, at] = x_ref[item, 0:TILE]
            ks[side, at] = x_ref[item, TILE : 2 * TILE]
            vs[side, at, :HD] = x_ref[item, 2 * TILE : 3 * TILE]
            return carry

        lax.fori_loop(0, far_tiles, one, 0)
        left_tiles = (left + TILE - 1) // TILE
        right_tiles = (right + TILE - 1) // TILE
        first = rows - TILE * left_tiles
        blocks = (TILE * (left_tiles + right_tiles) + BLK - 1) // BLK
        for n in range(1, rows // BLK + 2):

            @pl.when(blocks == n)
            def _(n=n):
                width = n * BLK
                whole = pl.ds(pl.multiple_of(first, TILE), width)
                k = ks[side, whole]
                v_ones = vs[side, whole]
                place = first + lax.broadcasted_iota(jnp.int32, (1, width), 1)
                valid = (place >= rows - left) & (place < rows + right)
                bias = jnp.where(valid, 0.0, NEG)
                for j in range(n):
                    at = pl.ds(pl.multiple_of(first + j * BLK, TILE), BLK)
                    o = attend_rows(qs[side, at], k, v_ones, lambda s: s + bias)
                    zs[side, at] += jnp.dot(o, w_ref[...], preferred_element_type=jnp.float32)
                    wide = o.astype(jnp.float32)
                    ss[side, at] += wide * wide

    @pl.when((h < scal[L_HEADS]) & (scal[L_TILES] > 0))
    def _():
        work(0, xl_ref, scal[L_TILES], h, rows, rows - TILE * scal[L_TILES], scal[L_FAR], scal[L_OWN])

    @pl.when((h >= scal[R_HEADS]) & (scal[R_TILES] > 0))
    def _():
        work(1, xr_ref, scal[R_TILES], h - scal[R_HEADS], 0, rows, scal[R_OWN], scal[R_FAR])

    @pl.when(h == pl.num_programs(0) - 1)
    def _():
        row = lax.broadcasted_iota(jnp.int32, (rows, HD), 0)
        low, high = slice(0, rows), slice(rows, 2 * rows)
        own_ref[...] = with_total(zs[0, high], ss[0, high], row < scal[L_OWN]) + with_total(
            zs[1, low], ss[1, low], row >= rows - scal[R_OWN]
        )
        toleft_ref[...] = with_total(zs[0, low], ss[0, low], row >= rows - scal[L_FAR])
        toright_ref[...] = with_total(zs[1, high], ss[1, high], row < scal[R_FAR])


def step_rows(video_ids, step_sizes):
    chosen = video_ids[:, None] == jnp.arange(step_sizes.shape[0], dtype=jnp.int32)[None, :]
    return jnp.sum(jnp.where(chosen, step_sizes[None, :], 0.0), axis=1)


def per_device(
    query_rows, key_rows, value_rows, positions, latents, w_head, modulation,
    guide_scale, step_sizes, lengths,
):
    rows, features = query_rows.shape[1], query_rows.shape[2]
    heads = features // HD
    count = lax.axis_size("req")
    row_count = rows * count
    here = lax.axis_index("req")
    first_row = here * rows
    cap = max(
        min(max(a * n, b * (heads - n)) for n in range(heads + 1))
        for a in range(1, rows // TILE + 1)
        for b in [rows // TILE + 1 - a]
    )
    cap = -(-cap // 2) * 2

    angle = angles(positions)
    odd = (jnp.arange(HD, dtype=jnp.int32) % 2).astype(jnp.float32)
    cosine = jnp.cos(angle)
    sine = jnp.sin(angle) * (2.0 * odd - 1.0)[None, :]

    ends = jnp.cumsum(lengths)
    starts = ends - lengths
    ll, lr, llt, lrt, ln = boundary(first_row, row_count, ends, starts, heads)
    rl, rr, rlt, rrt, rn = boundary(first_row + rows, row_count, ends, starts, heads)
    scalars = jnp.stack([llt, lrt, ln, ll, lr, rrt, rlt, rn, rr, rl]).astype(jnp.int32)

    q, k, v = query_rows[0], key_rows[0], value_rows[0]
    head_block = pl.BlockSpec((rows, HD), lambda h, s: (0, h))
    table = pl.BlockSpec((rows, HD), lambda h, s: (0, 0))
    w_block = pl.BlockSpec((HD, HD), lambda h, s: (h, 0))
    box = pl.BlockSpec((cap, 3 * TILE, HD), lambda h, s: (0, 0, 0))
    box_shape = jax.ShapeDtypeStruct((cap, 3 * TILE, HD), jnp.bfloat16)
    params = pltpu.CompilerParams(
        dimension_semantics=("arbitrary",), vmem_limit_bytes=VMEM_LIMIT
    )
    q_rot, k_rot, box_left, box_right = pl.pallas_call(
        prep_kernel,
        out_shape=(
            jax.ShapeDtypeStruct(q.shape, q.dtype), jax.ShapeDtypeStruct(k.shape, k.dtype),
            box_shape, box_shape,
        ),
        grid_spec=pltpu.PrefetchScalarGridSpec(
            num_scalar_prefetch=1, grid=(heads,),
            in_specs=[head_block] * 3 + [table] * 2,
            out_specs=[head_block] * 2 + [box] * 2,
        ),
        compiler_params=params,
        name="rotate_and_pack",
    )(scalars, q, k, v, cosine, sine)

    to_right = [(i, i + 1) for i in range(count - 1)]
    to_left = [(i + 1, i) for i in range(count - 1)]
    from_left = lax.ppermute(box_right, "req", to_right)
    from_right = lax.ppermute(box_left, "req", to_left)

    scaled = (1.0 + modulation[1])[:, None] * w_head.astype(jnp.float32)
    high = lax.reduce_precision(scaled, 8, 7)
    w_both = jnp.concatenate([high, scaled - high], axis=1).astype(jnp.bfloat16)
    shift = jnp.dot(
        modulation[0][None, :], w_head.astype(jnp.float32), precision=lax.Precision.HIGHEST
    )
    own_rows = first_row + jnp.arange(rows, dtype=jnp.int32)
    video = jnp.sum((ends[None, :] <= own_rows[:, None]).astype(jnp.int32), axis=1)

    local = pl.pallas_call(
        local_kernel,
        out_shape=jax.ShapeDtypeStruct((rows, HD), jnp.float32),
        grid_spec=pltpu.PrefetchScalarGridSpec(
            num_scalar_prefetch=1, grid=(heads,),
            in_specs=[head_block] * 3 + [
                w_block,
                pl.BlockSpec((rows, 1), lambda h, s: (0, 0)),
                pl.BlockSpec((1, rows), lambda h, s: (0, 0)),
            ],
            out_specs=table,
            scratch_shapes=[pltpu.VMEM((rows, HD), jnp.float32)] * 2,
        ),
        compiler_params=params,
        cost_estimate=pl.CostEstimate(
            flops=heads * rows * rows * HD * 4, bytes_accessed=3 * rows * features * 2,
            transcendentals=heads * rows * rows,
        ),
        name="inner_videos",
    )(scalars, q_rot, k_rot, v, w_both, video[:, None], video[None, :])

    span = 2 * rows + BLK
    own, ret_left, ret_right = pl.pallas_call(
        straddle_kernel,
        out_shape=(jax.ShapeDtypeStruct((rows, HD), jnp.float32),) * 3,
        grid_spec=pltpu.PrefetchScalarGridSpec(
            num_scalar_prefetch=1, grid=(heads,),
            in_specs=[head_block] * 3 + [box] * 2 + [w_block],
            out_specs=[table] * 3,
            scratch_shapes=[
                pltpu.VMEM((2, span, HD), jnp.bfloat16),
                pltpu.VMEM((2, span, HD), jnp.bfloat16),
                pltpu.VMEM((2, span, 2 * HD), jnp.bfloat16),
                pltpu.VMEM((2, span, HD), jnp.float32),
                pltpu.VMEM((2, span, HD), jnp.float32),
            ],
        ),
        compiler_params=params,
        name="videos_across",
    )(scalars, q_rot, k_rot, v, from_left, from_right, w_both)

    back_right = lax.ppermute(ret_left, "req", to_left)
    back_left = lax.ppermute(ret_right, "req", to_right)
    total = local + own + back_right + back_left
    half = HD // 2
    scale = lax.rsqrt(total[:, half : half + 1] / features + 1e-06)
    velocity = total[:, :half] * scale + shift

    parity = lax.axis_index("cfg")
    partner = lax.ppermute(velocity, "cfg", [(0, 1), (1, 0)])
    conditional = jnp.where(parity == 0, velocity, partner)
    unconditional = jnp.where(parity == 0, partner, velocity)
    guided = unconditional + guide_scale[0] * (conditional - unconditional)
    width = latents.shape[1]
    mine = lax.dynamic_slice_in_dim(guided, parity * width, width, 1)
    return latents + step_rows(video, step_sizes)[:, None] * mine


def solution(mesh):
    in_specs = (
        P("cfg", "req", None), P("cfg", "req", None), P("cfg", "req", None),
        P(None, "req"), P("req", "cfg"), P(), P(), P(), P(), P(),
    )
    return jax.shard_map(
        per_device, mesh=mesh, in_specs=in_specs, out_specs=P("req", "cfg"), check_vma=False
    )
```

time: 413 us -> 235 us (0.57); the launches traced: 410 us -> 239 us
  waiting for transfers between devices: 209 us -> 84.6 us
  Pallas kernels: 0 us -> 118 us
  matrix products: 70.5 us -> 0.34 us
  other arithmetic: 75.1 us -> 9.18 us
  local copies, waits for them, and re-layouts: 45.3 us -> 7.08 us
  starting transfers between devices: 8.86 us -> 16.3 us
    ppermute x3 -> x5, waiting for transfers between devices: 209 us -> 84.6 us  [the longest x1 82.6 us: per_device(): from_left = lax.ppermute(box_right, 'req', to_right)]
    pallas_call x0 -> x3, Pallas kernels: none -> 118 us  [the longest x1 60.8 us: per_device(): pl.pallas_call(straddle_kernel, out_shape=(jax.ShapeDtypeStruct((rows, HD...]
    dot_general x41 -> x1, matrix products: 70.5 us -> 0.34 us  [per_device(): jnp.dot(modulation[0][None, :], w_head.astype(jnp.float32), precision=lax...]
    convert_element_type x6 -> x0, local copies, waits for them, and re-layouts: 32.3 us -> none  [the longest x4 23.4 us: rotate(): features.astype(jnp.float32).reshape(row_total, heads_here, HD // 2, 2)]
    another operation x5, other arithmetic: 31 us -> 2.05 us  [the longest x2 1.45 us: boundary(): best = jnp.argmin(load).astype(jnp.int32)]
    concatenate x2 -> x1, other arithmetic: 28.1 us -> 1.19 us  [per_device(): w_both = jnp.concatenate([high, scaled - high], axis=1).astype(jnp.bfloat16)]
    reduce_sum x24 -> x3, other arithmetic: 12.4 us -> 1.6 us  [the longest x1 1.42 us: boundary(): left = jnp.sum(jnp.where(inside, at - starts, 0))]
    ppermute x3 -> x5, starting transfers between devices: 8.86 us -> 16.3 us  [the longest x1 5.16 us: per_device(): back_right = lax.ppermute(ret_left, 'req', to_left)]
  transfers between devices with their start and end apart: 3 -> 5, of which waited for: 3 -> 3; matrix products, arithmetic and copies ran while one was open for 3% -> 1% of each run, Pallas kernels for 0% -> 16%
where the time goes in v1:
time: 235 us; the launch traced here: 239 us
  Pallas kernels  118 us (50%)
  waiting for transfers between devices  84.6 us (36%)
  starting transfers between devices  16.3 us (7%)
  other arithmetic  9.18 us (4%)
  local copies, waits for them, and re-layouts  7.08 us (3%)
  between operations  3.46 us (1%)
    ppermute x1, waiting for transfers between devices, per_device(): from_left = lax.ppermute(box_right, 'req', to_right)  82.6 us
    pallas_call x1, Pallas kernels, per_device(): pl.pallas_call(straddle_kernel, out_shape=(jax.ShapeDtypeStruct((rows, HD...  60.8 us
    pallas_call x1, Pallas kernels, per_device(): pl.pallas_call(local_kernel, out_shape=jax.ShapeDtypeStruct((rows, HD), j...  38.8 us
    pallas_call x1, Pallas kernels, per_device(): pl.pallas_call(prep_kernel, out_shape=(jax.ShapeDtypeStruct(q.shape, q.dt...  18.8 us
    ppermute x1, starting transfers between devices, per_device(): back_right = lax.ppermute(ret_left, 'req', to_left)  5.16 us
  transfers between devices with their start and end apart: 5, of which 3 were waited for; matrix products, arithmetic and copies ran while one was open for 1% of the time, Pallas kernels for 16%

profile of v1, /device:TPU:17, one launch (start us, length us, event | category | flops | bytes accessed | tf_op | source)
XLA Modules:
  0.0 239.3 jit_solution(3895295017511466586)
XLA Ops:
  0.0 0.7 copy.25
  0.9 1.4 select_reduce_fusion.1
  5.0 0.7 convert_element_type.34
  5.7 0.7 iota_reduce_fusion.1
  6.4 0.7 iota_reduce_fusion
  7.2 1.9 sine_multiply_fusion
  9.1 4.2 %stack.49.scal = s32[10]{0:T(128)} concatenate(s32[1]{0:T(128)} %bitcast.1, s32[1]{0:T(128)} %bitcast.2, s32[1]{0:T(128)} %bitcast.3, s32[1]{0:T(128)} %bitcast.4, s32[1]{0:T(128)} %bitcast.5, s32[1]{0:T(128)} %bitcast.6, s32[1]{0:T(128)} %bitcast.7, s32[1]{0:T(128)} %bitcast.8, s32[1]{0:T(128)} %bitcast.9, s32[1]{0:T(128)} %bitcast.10), dimensions={0} | concatenate | bytes 80 | tf_op jit(solution)/shard_map/stack | solution.py:241
  13.3 18.8 %rotate_and_pack.1 = (bf16[512,2560]{1,0:T(8,128)(2,1)}, bf16[512,2560]{1,0:T(8,128)(2,1)}, bf16[170,48,128]{2,1,0:T(8,128)(2,1)}, bf16[170,48,128]{2,1,0:T(8,128)(2,1)}) custom-call(s32[10]{0:T(128)} %stack.49.scal, bf16[512,2560]{1,0:T(8,128)(2,1)} %bitcast.36, bf16[512,2560]{1,0:T(8,128)(2,1)} %bitcast.37, bf16[512,2560]{1,0:T(8,128)(2,1)} %bitcast.33, ...), custom_call_target="tpu_custom_call" | custom-call | tf_op jit(solution)/shard_map/rotate_and_pack/pallas_call | solution.py:252
  32.1 2.9 %collective-permute-start = (bf16[170,48,128]{2,1,0:T(8,128)(2,1)}, bf16[170,48,128]{2,1,0:T(8,128)(2,1)S(1)}, u32[]{:S(2)}, u32[]{:S(2)}) collective-permute-start(bf16[170,48,128]{2,1,0:T(8,128)(2,1)} %get-tuple-element.18), channel_id=1, source_target_pairs={{0,1},{1,2},{2,3},{3,4},{4,5},{5,6},{6,7},{7,8},{8,9},{9,10},{10,1... | collective-permute-start | bytes 6266888 | tf_op jit(solution)/shard_map/ppermute | solution.py:269
  35.0 4.2 %collective-permute-start.1 = (bf16[170,48,128]{2,1,0:T(8,128)(2,1)}, bf16[170,48,128]{2,1,0:T(8,128)(2,1)}, u32[]{:S(2)}, u32[]{:S(2)}) collective-permute-start(bf16[170,48,128]{2,1,0:T(8,128)(2,1)} %get-tuple-element.19), channel_id=1, source_target_pairs={{1,0},{2,1},{3,2},{4,3},{5,4},{6,5},{7,6},{8,7},{9,8},{10,9},{11,1... | collective-permute-start | bytes 6266888 | tf_op jit(solution)/shard_map/ppermute | solution.py:270
  39.2 0.3 copy.26
  39.6 0.3 convolution_bitcast_fusion
  39.9 0.4 reduce-precision_convert_fusion
  40.4 1.2 pad_maximum_fusion.w_ref
  41.6 82.6 %collective-permute-done.xl_ref = bf16[170,48,128]{2,1,0:T(8,128)(2,1)S(1)} collective-permute-done((bf16[170,48,128]{2,1,0:T(8,128)(2,1)}, bf16[170,48,128]{2,1,0:T(8,128)(2,1)S(1)}, u32[]{:S(2)}, u32[]{:S(2)}) %collective-permute-start) | collective-permute-done | bytes 2088992 | tf_op jit(solution)/shard_map/ppermute | solution.py:269
  124.2 1.7 collective-permute-done.1.xr_ref
  125.9 60.8 %videos_across.1 = (f32[512,128]{1,0:T(8,128)}, f32[512,128]{1,0:T(8,128)}, f32[512,128]{1,0:T(8,128)}) custom-call(s32[10]{0:T(128)} %stack.49.scal, bf16[512,2560]{1,0:T(8,128)(2,1)} %get-tuple-element.16.q_ref, bf16[512,2560]{1,0:T(8,128)(2,1)} %get-tuple-element.17.k_ref, bf16[512,2560]{1,0:T(8,128)(2,1)} %bitcast.34, bf16[170,48,128]{2,1,0:T(8,128)(2,1)} %copy-done, ...), custom_call_target="tpu_custom_call" | custom-call | tf_op jit(solution)/shard_map/videos_across/pallas_call | solution.py:303
  186.7 1.9 collective-permute-start.3
  188.6 5.2 %collective-permute-start.2 = (f32[512,128]{1,0:T(8,128)}, f32[512,128]{1,0:T(8,128)S(1)}, u32[]{:S(2)}, u32[]{:S(2)}) collective-permute-start(f32[512,128]{1,0:T(8,128)} %get-tuple-element.21), channel_id=1, source_target_pairs={{1,0},{2,1},{3,2},{4,3},{5,4},{6,5},{7,6},{8,7},{9,8},{10,9},{11,1... | collective-permute-start | bytes 786440 | tf_op jit(solution)/shard_map/ppermute | solution.py:322
  193.8 0.9 copy.28.qv_ref
  194.7 38.8 %inner_videos.1 = f32[512,128]{1,0:T(8,128)} custom-call(s32[10]{0:T(128)} %stack.49.scal, bf16[512,2560]{1,0:T(8,128)(2,1)} %get-tuple-element.16.q_ref, bf16[512,2560]{1,0:T(8,128)(2,1)} %get-tuple-element.17.k_ref, bf16[512,2560]{1,0:T(8,128)(2,1)} %bitcast.35, bf16[2560,128]{1,0:T(8,128)(2,1)} %pad_maximum_fusion.w_ref, s32[512,1]{1,0:T(8,128)} %copy.28.qv_ref, ...), custom_call_target="tpu_custom_call" | custom-call | flops 2684354560 | bytes 7864320 | tf_op jit(solution)/shard_map/inner_videos/pallas_call | solution.py:281
  233.6 1.0 add_add_fusion
  235.0 2.2 collective-permute-start.4
  238.6 0.7 copy.31
  (35 shorter events, 1.5 us)
Async XLA Ops:
  13.3 25.9 %copy-start.1 = (bf16[2560,64]{0,1:T(8,128)(2,1)S(1)}, bf16[2560,64]{0,1:T(8,128)(2,1)}, u32[]{:S(2)}) copy-start(bf16[2560,64]{0,1:T(8,128)(2,1)} %param.15) | copy-start | bytes 983044
  13.3 26.2 %copy-start.6 = (f32[2,2560]{1,0:T(2,128)S(1)}, f32[2,2560]{1,0:T(2,128)}, u32[]{:S(2)}) copy-start(f32[2,2560]{1,0:T(2,128)} %param.16) | copy-start | bytes 61444
  32.1 92.1 %collective-permute-start = (bf16[170,48,128]{2,1,0:T(8,128)(2,1)}, bf16[170,48,128]{2,1,0:T(8,128)(2,1)S(1)}, u32[]{:S(2)}, u32[]{:S(2)}) collective-permute-start(bf16[170,48,128]{2,1,0:T(8,128)(2,1)} %get-tuple-element.18), channel_id=1, source_target_pairs={{0,1},{1,2},{2,3},{3,4},{4,5},{5,6},{6,7},{7,8},{8,9},{9,10},{10,1... | collective-permute-start | bytes 6266888 | tf_op jit(solution)/shard_map/ppermute | solution.py:269
  35.0 90.9 %collective-permute-start.1 = (bf16[170,48,128]{2,1,0:T(8,128)(2,1)}, bf16[170,48,128]{2,1,0:T(8,128)(2,1)}, u32[]{:S(2)}, u32[]{:S(2)}) collective-permute-start(bf16[170,48,128]{2,1,0:T(8,128)(2,1)} %get-tuple-element.19), channel_id=1, source_target_pairs={{1,0},{2,1},{3,2},{4,3},{5,4},{6,5},{7,6},{8,7},{9,8},{10,9},{11,1... | collective-permute-start | bytes 6266888 | tf_op jit(solution)/shard_map/ppermute | solution.py:270
  124.2 1.7 copy-start
  186.7 46.9 %collective-permute-start.3 = (f32[512,128]{1,0:T(8,128)}, f32[512,128]{1,0:T(8,128)S(1)}, u32[]{:S(2)}, u32[]{:S(2)}) collective-permute-start(f32[512,128]{1,0:T(8,128)} %get-tuple-element.22), channel_id=1, source_target_pairs={{0,1},{1,2},{2,3},{3,4},{4,5},{5,6},{6,7},{7,8},{8,9},{9,10},{10,1... | collective-permute-start | bytes 786440 | tf_op jit(solution)/shard_map/ppermute | solution.py:323
  188.6 45.0 %collective-permute-start.2 = (f32[512,128]{1,0:T(8,128)}, f32[512,128]{1,0:T(8,128)S(1)}, u32[]{:S(2)}, u32[]{:S(2)}) collective-permute-start(f32[512,128]{1,0:T(8,128)} %get-tuple-element.21), channel_id=1, source_target_pairs={{1,0},{2,1},{3,2},{4,3},{5,4},{6,5},{7,6},{8,7},{9,8},{10,9},{11,1... | collective-permute-start | bytes 786440 | tf_op jit(solution)/shard_map/ppermute | solution.py:322
  193.8 0.9 copy-start.4
  194.7 38.9 %copy-start.2 = (f32[512,128]{1,0:T(8,128)S(1)}, f32[512,128]{1,0:T(8,128)}, u32[]{:S(2)}) copy-start(f32[512,128]{1,0:T(8,128)} %get-tuple-element.20) | copy-start | bytes 786436
  233.5 3.6 %copy-start.3 = (f32[512,32]{0,1:T(8,128)S(1)}, f32[512,32]{0,1:T(8,128)}, u32[]{:S(2)}) copy-start(f32[512,32]{0,1:T(8,128)} %param.14) | copy-start | bytes 196612
  233.5 4.4 %copy-start.5 = (s32[512]{0:T(512)S(1)}, s32[512]{0:T(512)}, u32[]{:S(2)}) copy-start(s32[512]{0:T(512)} %copy-done.4) | copy-start | bytes 6148
  233.5 4.4 %copy-start.7 = (f32[32]{0:T(128)S(1)}, f32[32]{0:T(128)}, u32[]{:S(2)}) copy-start(f32[32]{0:T(128)} %param.18) | copy-start | bytes 388
  235.0 3.3 %collective-permute-start.4 = (f32[512,64]{1,0:T(8,128)S(1)}, f32[512,64]{1,0:T(8,128)S(1)}, u32[]{:S(2)}, u32[]{:S(2)}) collective-permute-start(f32[512,64]{1,0:T(8,128)S(1)} %fusion.4), channel_id=1, source_target_pairs={{0,16},{16,0},{1,17},{17,1},{2,18},{18,2},{3,19},{19,3},{4,20},{20... | collective-permute-start | bytes 393224 | tf_op jit(solution)/shard_map/ppermute | solution.py:330
